TPU v7x, 256 devices: a whole 4x4x8 slice. The times are simulated.
256 devices in a mesh: gx: 16 (over y, x), gy: 16 (over z, core).
Axes of the slice: x: 4, y: 4, z: 8, core: 2. Of those that a mesh axis runs over, the one named last changes fastest.
Arguments:
- vectors: float32 [8, 128, 256, 256], P(None, 'gx', 'gy'), may hold values from -10 to 10
- weight_x: float32 [128, 256, 256], P('gx', 'gy'), may hold values from 0.05 to 1
- weight_y: float32 [128, 256, 256], P('gx', 'gy'), may hold values from 0.05 to 1
- weight_z: float32 [128, 256, 256], P('gx', 'gy'), may hold values from 0.05 to 1
Outputs:
- refined: float32 [8, 128, 256, 256], P(None, 'gx', 'gy')
- eigenvalues: float32 [8], replicated
All inputs are finite; a program needn't handle non-finite values.
Results may differ from a plain program's by a relative error of at most 0.000075.
Values sent between devices are 32-bit elements; how exact they have to be, the bound alone decides.
No kernel may reach another device: no remote copies, remote signals or barrier semaphores. Data moves between devices by JAX's collectives and lax.ppermute only.
A program may use at most 128 MiB of HBM per device.

v0:
```python
import jax
import jax.numpy as jnp
from jax import lax
from jax.sharding import PartitionSpec as P

COARSE_SWEEPS = 4
OMEGA = 0.8
SHIFT = 0.1


def shifted(shard, axis, by):
    count = lax.axis_size(axis)
    pairs = [(i, i + by) for i in range(count) if 0 <= i + by < count]
    return lax.ppermute(shard, axis, pairs)


def with_halo(cells, sides, width):
    for axis, dim in sides:
        count = lax.axis_size(axis)
        ends = count - 1
        head = lax.slice_in_dim(cells, 0, width, axis=dim)
        tail = lax.slice_in_dim(cells, cells.shape[dim] - width, cells.shape[dim], axis=dim)
        cells = jnp.concatenate(
            [
                lax.ppermute(tail, axis, [(i, (i + 1) % count) for i in range(ends)]),
                cells,
                lax.ppermute(head, axis, [((i + 1) % count, i) for i in range(ends)]),
            ],
            axis=dim,
        )
    return cells


def lower_x(weights):
    rim = shifted(weights[-1:], "gx", 1)
    return jnp.concatenate([rim, weights[:-1]], 0)


def lower_y(weights):
    rim = shifted(weights[:, -1:], "gy", 1)
    return jnp.concatenate([rim, weights[:, :-1]], 1)


def lower_z(weights):
    return jnp.concatenate([jnp.zeros_like(weights[:, :, :1]), weights[:, :, :-1]], 2)


def trimmed(array):
    return array[..., 1:-1, 1:-1, :]


def inner_sum(field, parts):
    wx, lx, wy, ly, wz, lz = parts
    centre = trimmed(field)
    zpadded = jnp.pad(centre, ((0, 0), (0, 0), (0, 0), (1, 1)))
    total = wx[None] * field[:, 2:, 1:-1] + lx[None] * field[:, :-2, 1:-1]
    total = total + wy[None] * field[:, 1:-1, 2:] + ly[None] * field[:, 1:-1, :-2]
    total = total + wz[None] * zpadded[..., 2:] + lz[None] * zpadded[..., :-2]
    return total


def neighbours(field, parts, level):
    if level == "fine":
        padded = with_halo(field, (("gx", 1), ("gy", 2)), 1)
    else:
        padded = with_halo(field, (("gx", 1), ("gy", 2)), 1)
    return inner_sum(padded, parts)


def jacobi(guess, source, diag, parts, level):
    return (
        guess
        + OMEGA * (source - (diag[None] * guess - neighbours(guess, parts, level))) / diag[None]
    )


def rayleigh_sums(vectors, applied, degree):
    return lax.psum(
        (
            jnp.sum(vectors * applied, axis=(1, 2, 3)),
            jnp.sum(vectors * (degree[None] * vectors), axis=(1, 2, 3)),
        ),
        ("gx", "gy"),
    )


def coarse_weights(wx, wy, wz, degree):
    sx, sy, sz = wx.shape
    shape = (sx // 2, 2, sy // 2, 2, sz // 2, 2)
    cx = wx.reshape(shape)[:, 1].sum(axis=(2, 4))
    cy = wy.reshape(shape)[:, :, :, 1].sum(axis=(1, 4))
    cz = wz.reshape(shape)[..., 1].sum(axis=(1, 3))
    dsum = degree.reshape(shape).sum(axis=(1, 3, 5))
    return (cx, cy, cz, dsum)


def restrict(field):
    kk, sx, sy, sz = field.shape
    return field.reshape(kk, sx // 2, 2, sy // 2, 2, sz // 2, 2).sum(axis=(2, 4, 6))


def prolong(field):
    kk, sx, sy, sz = field.shape
    return jnp.broadcast_to(field[:, :, None, :, None, :, None], (kk, sx, 2, sy, 2, sz, 2)).reshape(
        kk, 2 * sx, 2 * sy, 2 * sz
    )


def per_device(vectors, weight_x, weight_y, weight_z):
    local_x, local_y, depth = weight_x.shape
    span_x = local_x * lax.axis_size("gx")
    span_y = local_y * lax.axis_size("gy")
    pos_x = lax.axis_index("gx") * local_x + lax.broadcasted_iota(jnp.int32, (local_x, 1, 1), 0)
    pos_y = lax.axis_index("gy") * local_y + lax.broadcasted_iota(jnp.int32, (1, local_y, 1), 1)
    pos_z = lax.broadcasted_iota(jnp.int32, (1, 1, depth), 2)
    wx = jnp.where(pos_x < span_x - 1, weight_x, jnp.zeros_like(weight_x))
    wy = jnp.where(pos_y < span_y - 1, weight_y, jnp.zeros_like(weight_y))
    wz = jnp.where(pos_z < depth - 1, weight_z, jnp.zeros_like(weight_z))
    parts = (wx, lower_x(wx), wy, lower_y(wy), wz, lower_z(wz))
    degree = parts[0] + parts[1] + parts[2] + parts[3] + parts[4] + parts[5]
    applied = degree[None] * vectors - neighbours(vectors, parts, "fine")
    numer, denom = rayleigh_sums(vectors, applied, degree)
    eigenvalues = numer / denom
    resid = applied - eigenvalues[:, None, None, None] * (degree[None] * vectors)
    dfine = (1.0 + SHIFT) * degree
    guess = OMEGA * resid / dfine[None]
    guess = jacobi(guess, resid, dfine, parts, "fine")
    fine_rest = resid - (dfine[None] * guess - neighbours(guess, parts, "fine"))
    cx, cy, cz, dsum = coarse_weights(wx, wy, wz, degree)
    cparts = (cx, lower_x(cx), cy, lower_y(cy), cz, lower_z(cz))
    dcoarse = cparts[0] + cparts[1] + cparts[2] + cparts[3] + cparts[4] + cparts[5] + SHIFT * dsum
    rcoarse = restrict(fine_rest)
    correction = OMEGA * rcoarse / dcoarse[None]
    for sweep in range(COARSE_SWEEPS - 1):
        correction = jacobi(correction, rcoarse, dcoarse, cparts, "coarse")
    guess = guess + prolong(correction)
    guess = jacobi(guess, resid, dfine, parts, "fine")
    updated = vectors - guess
    local_gram = jnp.einsum(
        "aijk,bijk->ab", updated, degree[None] * updated, precision=lax.Precision.HIGHEST
    )
    gram = lax.psum(local_gram, ("gx", "gy"))
    gram = gram / (span_x * span_y * depth)
    chol = jnp.linalg.cholesky(gram)
    flat = updated.reshape(updated.shape[0], -1)
    refined = jax.scipy.linalg.solve_triangular(chol, flat, lower=True).reshape(updated.shape)
    return (refined, eigenvalues)


def solution(mesh):
    return jax.shard_map(
        per_device,
        mesh=mesh,
        in_specs=(
            P(None, "gx", "gy", None),
            P("gx", "gy", None),
            P("gx", "gy", None),
            P("gx", "gy", None),
        ),
        out_specs=(P(None, "gx", "gy", None), P()),
        check_vma=False,
    )
```

profile of v0, /device:TPU:1, one launch (start us, length us, event | category | flops | bytes accessed | tf_op | source)
XLA Modules:
  0.0 427.5 jit_solution(8508537190117706973)
XLA Ops:
  1.7 3.9 collective-permute-start
  6.6 4.4 %collective-permute-start.1 = (f32[8,1,256]{2,1,0:T(1,128)S(1)}, f32[8,1,256]{2,1,0:T(1,128)S(1)}, u32[]{:S(2)}, u32[]{:S(2)}) collective-permute-start(f32[8,1,256]{2,1,0:T(1,128)S(1)} %slice.374), channel_id=1, source_target_pairs={{0,1},{1,2},{2,3},{3,4},{4,5},{5,6},{6,7},{7,8},{8,9},{9,10},{10,1... | collective-permute-start | bytes 24584 | tf_op jit(solution)/shard_map/ppermute | solution.py:14
  12.0 3.1 collective-permute-start.3
  16.5 9.8 %reshape.74 = f32[4,2,8,2,128,2]{5,4,3,2,1,0:T(8,128)} reshape(f32[8,16,256]{2,1,0:T(8,128)S(1)} %broadcast_select_fusion.2) | data formatting | bytes 262144 | tf_op jit(solution)/shard_map/reshape | solution.py:90
  26.6 1.9 collective-permute-start.4
  28.6 3.6 collective-permute-start.5
  33.8 2.1 fusion
  35.9 82.2 %all-reduce.9 = (f32[8]{0:T(128)S(1)}, f32[8]{0:T(128)S(1)}) all-reduce(f32[8]{0:T(128)S(1)} %get-tuple-element.19, f32[8]{0:T(128)S(1)} %get-tuple-element.18), channel_id=1, replica_groups=mesh['gx'=16,'gy'=16] {'gx','gy'}, use_global_device_ids=true, to_apply=%region_1.2 | all-reduce | flops 16 | bytes 128 | tf_op jit(solution)/shard_map/psum | solution.py:78
  118.1 1.7 multiply_divide_fusion
  121.8 4.7 %collective-permute-start.7 = (f32[8,1,16,256]{3,2,1,0:T(8,128)}, f32[8,1,16,256]{3,2,1,0:T(8,128)}, u32[]{:S(2)}, u32[]{:S(2)}) collective-permute-start(f32[8,1,16,256]{3,2,1,0:T(8,128)} %get-tuple-element.44), channel_id=1, source_target_pairs={{0,16},{16,32},{32,48},{48,64},{64,80},{80,96},{96,112},{112,128},... | collective-permute-start | bytes 393224 | tf_op jit(solution)/shard_map/ppermute | solution.py:25
  126.5 2.8 slice_reduce_fusion.2
  130.5 2.5 collective-permute-start.14
  133.0 9.7 %reshape.75 = f32[4,2,8,2,128,2]{5,4,3,2,1,0:T(8,128)} reshape(f32[8,16,256]{2,1,0:T(8,128)S(1)} %broadcast_select_fusion.1) | data formatting | bytes 262144 | tf_op jit(solution)/shard_map/reshape | solution.py:91
  143.8 3.4 collective-permute-start.8
  147.2 2.9 collective-permute-start.9
  150.1 2.8 slice_reduce_fusion.1
  153.5 2.5 collective-permute-start.15
  156.1 9.8 %reshape.76 = f32[4,2,8,2,128,2]{5,4,3,2,1,0:T(8,128)} reshape(f32[8,16,256]{2,1,0:T(8,128)S(1)} %broadcast_select_fusion) | data formatting | bytes 262144 | tf_op jit(solution)/shard_map/reshape | solution.py:92
  166.1 5.3 %fusion.13 = f32[8,8,16,256]{3,2,1,0:T(8,128)S(1)} fusion(f32[8,8,16,256]{3,2,1,0:T(8,128)} %copy-done.1, f32[8,8,16,256]{3,2,1,0:T(8,128)S(1)} %get-tuple-element.27, f32[8,10,1,256]{3,2,1,0:T(1,128)S(1)} %copy.441, f32[8,1,16,256]{3,2,1,0:T(8,128)} %copy-done.25, f32[8,1,16,256]{3,2,1,0:T(8,128)} %collective-permute-done.7, ...), kind=kLoop, calls=%fused_computation.28 | loop fusion | flops 6553600 | bytes 4489216 | tf_op jit(solution)/shard_map/add | solution.py:72
  173.4 4.7 %collective-permute-start.11 = (f32[8,1,16,256]{3,2,1,0:T(8,128)}, f32[8,1,16,256]{3,2,1,0:T(8,128)}, u32[]{:S(2)}, u32[]{:S(2)}) collective-permute-start(f32[8,1,16,256]{3,2,1,0:T(8,128)} %get-tuple-element.42), channel_id=1, source_target_pairs={{0,16},{16,32},{32,48},{48,64},{64,80},{80,96},{96,112},{112,128},... | collective-permute-start | bytes 393224 | tf_op jit(solution)/shard_map/ppermute | solution.py:25
  178.1 6.8 %slice_reduce_fusion = f32[4,8,128]{2,1,0:T(8,128)} fusion(f32[4,2,8,2,128,2]{5,4,3,2,1,0:T(8,128)} %reshape.76), kind=kLoop, calls=%fused_computation | loop fusion | flops 12288 | bytes 81920 | tf_op jit(solution)/shard_map/reduce_sum | solution.py:92
  184.8 10.5 %reshape.77 = f32[4,2,8,2,128,2]{5,4,3,2,1,0:T(8,128)} reshape(f32[8,16,256]{2,1,0:T(8,128)} %copy-done.8) | data formatting | bytes 262144 | tf_op jit(solution)/shard_map/reshape | solution.py:93
  195.3 4.6 %reduce_sum.69 = f32[4,8,128]{2,1,0:T(8,128)} reduce(f32[4,2,8,2,128,2]{5,4,3,2,1,0:T(8,128)} %reshape.77, f32[]{:T(128)} %constant.65.clone.1), dimensions={1,3,5}, to_apply=%region_8.9 | reduce | flops 28672 | bytes 147460 | tf_op jit(solution)/shard_map/reduce_sum | solution.py:93
  201.2 3.0 collective-permute-start.12
  204.3 2.5 collective-permute-start.13
  208.5 2.8 fusion.19
  211.3 9.8 %copy.446 = f32[8,8,16,256]{0,3,2,1:T(8,128)} copy(f32[8,8,16,256]{3,2,1,0:T(8,128)} %fusion.19) | data formatting | bytes 2097152 | tf_op jit(solution)/shard_map/sub | solution.py:128
  221.1 13.1 %reduce_sum.65 = f32[8,4,8,128]{0,3,2,1:T(8,128)} reduce(f32[8,4,2,8,2,128,2]{0,6,5,4,3,2,1:T(2,128)} %bitcast.30, f32[]{:T(128)} %constant.65.clone.1), dimensions={2,4,6}, to_apply=%region_4.5 | reduce | flops 229376 | bytes 1179652 | tf_op jit(solution)/shard_map/reduce_sum | solution.py:99
  234.2 2.8 copy.447
  239.4 4.0 collective-permute-start.17
  244.4 2.9 collective-permute-start.18
  247.4 4.3 %collective-permute-start.19 = (f32[8,6,1,128]{3,2,1,0:T(1,128)S(1)}, f32[8,6,1,128]{3,2,1,0:T(1,128)S(1)}, u32[]{:S(2)}, u32[]{:S(2)}) collective-permute-start(f32[8,6,1,128]{3,2,1,0:T(1,128)S(1)} %get-tuple-element.53), channel_id=1, source_target_pairs={{0,1},{1,2},{2,3},{3,4},{4,5},{5,6},{6,7},{7,8},{8,9},{9,10},{10,1... | collective-permute-start | bytes 73736 | tf_op jit(solution)/shard_map/ppermute | solution.py:25
  255.1 4.6 %collective-permute-start.21 = (f32[8,1,8,128]{3,2,1,0:T(8,128)S(1)}, f32[8,1,8,128]{3,2,1,0:T(8,128)S(1)}, u32[]{:S(2)}, u32[]{:S(2)}) collective-permute-start(f32[8,1,8,128]{3,2,1,0:T(8,128)S(1)} %get-tuple-element.56), channel_id=1, source_target_pairs={{0,16},{16,32},{32,48},{48,64},{64,80},{80,96},{96,112},{112,128},... | collective-permute-start | bytes 98312 | tf_op jit(solution)/shard_map/ppermute | solution.py:25
  260.7 1.9 collective-permute-start.22
  262.6 5.1 %collective-permute-start.23 = (f32[8,6,1,128]{3,2,1,0:T(1,128)S(1)}, f32[8,6,1,128]{3,2,1,0:T(1,128)S(1)}, u32[]{:S(2)}, u32[]{:S(2)}) collective-permute-start(f32[8,6,1,128]{3,2,1,0:T(1,128)S(1)} %get-tuple-element.51), channel_id=1, source_target_pairs={{0,1},{1,2},{2,3},{3,4},{4,5},{5,6},{6,7},{7,8},{8,9},{9,10},{10,1... | collective-permute-start | bytes 73736 | tf_op jit(solution)/shard_map/ppermute | solution.py:25
  270.1 4.6 %collective-permute-start.25 = (f32[8,1,8,128]{3,2,1,0:T(8,128)S(1)}, f32[8,1,8,128]{3,2,1,0:T(8,128)S(1)}, u32[]{:S(2)}, u32[]{:S(2)}) collective-permute-start(f32[8,1,8,128]{3,2,1,0:T(8,128)S(1)} %get-tuple-element.54), channel_id=1, source_target_pairs={{0,16},{16,32},{32,48},{48,64},{64,80},{80,96},{96,112},{112,128},... | collective-permute-start | bytes 98312 | tf_op jit(solution)/shard_map/ppermute | solution.py:25
  275.8 1.9 collective-permute-start.26
  277.7 5.1 %collective-permute-start.27 = (f32[8,6,1,128]{3,2,1,0:T(1,128)S(1)}, f32[8,6,1,128]{3,2,1,0:T(1,128)S(1)}, u32[]{:S(2)}, u32[]{:S(2)}) collective-permute-start(f32[8,6,1,128]{3,2,1,0:T(1,128)S(1)} %get-tuple-element.49), channel_id=1, source_target_pairs={{0,1},{1,2},{2,3},{3,4},{4,5},{5,6},{6,7},{7,8},{8,9},{9,10},{10,1... | collective-permute-start | bytes 73736 | tf_op jit(solution)/shard_map/ppermute | solution.py:25
  284.5 2.9 copy.451
  287.4 7.1 %broadcast_in_dim.30 = f32[8,4,2,8,2,128,2]{0,6,5,4,3,2,1:T(2,128)} broadcast(f32[8,4,8,128]{0,3,2,1:T(8,128)} %copy.451), dimensions={0,1,3,5} | broadcast | bytes 1179648 | tf_op jit(solution)/shard_map/broadcast_in_dim | solution.py:104
  294.5 10.6 %copy.452 = f32[8,8,16,256]{3,2,1,0:T(8,128)} copy(f32[8,8,16,256]{0,3,2,1:T(8,128)} %bitcast.31) | data formatting | bytes 2097152 | tf_op jit(solution)/shard_map/reshape | solution.py:104
  308.1 4.6 %collective-permute-start.29 = (f32[8,1,16,256]{3,2,1,0:T(8,128)S(1)}, f32[8,1,16,256]{3,2,1,0:T(8,128)S(1)}, u32[]{:S(2)}, u32[]{:S(2)}) collective-permute-start(f32[8,1,16,256]{3,2,1,0:T(8,128)S(1)} %get-tuple-element.40), channel_id=1, source_target_pairs={{0,16},{16,32},{32,48},{48,64},{64,80},{80,96},{96,112},{112,128},... | collective-permute-start | bytes 393224 | tf_op jit(solution)/shard_map/ppermute | solution.py:25
  313.1 1.5 collective-permute-done.29
  314.7 1.9 collective-permute-start.30
  316.7 5.3 %collective-permute-start.31 = (f32[8,10,1,256]{3,0,2,1:T(8,128)S(1)}, f32[8,10,1,256]{3,0,2,1:T(8,128)S(1)}, u32[]{:S(2)}, u32[]{:S(2)}) collective-permute-start(f32[8,10,1,256]{3,0,2,1:T(8,128)S(1)} %copy.455), channel_id=1, source_target_pairs={{0,1},{1,2},{2,3},{3,4},{4,5},{5,6},{6,7},{7,8},{8,9},{9,10},{10,1... | collective-permute-start | bytes 245768 | tf_op jit(solution)/shard_map/ppermute | solution.py:25
  323.3 1.6 broadcast_multiply_fusion
  324.9 3.0 convolution_bitcast_fusion
  327.9 93.9 %psum.23 = f32[8,8]{0,1:T(8,128)S(1)} all-reduce(f32[8,8]{0,1:T(8,128)S(1)} %convolution_bitcast_fusion), channel_id=1, replica_groups=mesh['gx'=16,'gy'=16] {'gx','gy'}, use_global_device_ids=true, to_apply=%region_9.10 | all-reduce | flops 64 | bytes 512 | tf_op jit(solution)/shard_map/psum | solution.py:142
  (174 shorter events, 39.2 us)
Async XLA Ops:
  1.6 24.6 %copy-start.2 = (f32[8,16,256]{2,1,0:T(8,128)}, f32[8,16,256]{2,1,0:T(8,128)S(1)}, u32[]{:S(2)}) copy-start(f32[8,16,256]{2,1,0:T(8,128)S(1)} %broadcast_select_fusion.2) | copy-start | bytes 393220
  1.7 30.6 %collective-permute-start = (f32[1,16,256]{2,1,0:T(8,128)S(1)}, f32[1,16,256]{2,1,0:T(8,128)S(1)}, u32[]{:S(2)}, u32[]{:S(2)}) collective-permute-start(f32[1,16,256]{2,1,0:T(8,128)S(1)} %slice.372), channel_id=1, source_target_pairs={{0,16},{16,32},{32,48},{48,64},{64,80},{80,96},{96,112},{112,128},... | collective-permute-start | bytes 49160 | tf_op jit(solution)/shard_map/ppermute | solution.py:14
  6.6 25.6 %collective-permute-start.1 = (f32[8,1,256]{2,1,0:T(1,128)S(1)}, f32[8,1,256]{2,1,0:T(1,128)S(1)}, u32[]{:S(2)}, u32[]{:S(2)}) collective-permute-start(f32[8,1,256]{2,1,0:T(1,128)S(1)} %slice.374), channel_id=1, source_target_pairs={{0,1},{1,2},{2,3},{3,4},{4,5},{5,6},{6,7},{7,8},{8,9},{9,10},{10,1... | collective-permute-start | bytes 24584 | tf_op jit(solution)/shard_map/ppermute | solution.py:14
  12.0 14.3 %collective-permute-start.3 = (f32[8,1,16,256]{3,2,1,0:T(8,128)S(1)}, f32[8,1,16,256]{3,2,1,0:T(8,128)S(1)}, u32[]{:S(2)}, u32[]{:S(2)}) collective-permute-start(f32[8,1,16,256]{3,2,1,0:T(8,128)S(1)} %get-tuple-element.47), channel_id=1, source_target_pairs={{0,16},{16,32},{32,48},{48,64},{64,80},{80,96},{96,112},{112,128},... | collective-permute-start | bytes 393224 | tf_op jit(solution)/shard_map/ppermute | solution.py:25
  15.2 11.3 %collective-permute-start.2 = (f32[8,1,16,256]{3,2,1,0:T(8,128)S(1)}, f32[8,1,16,256]{3,2,1,0:T(8,128)S(1)}, u32[]{:S(2)}, u32[]{:S(2)}) collective-permute-start(f32[8,1,16,256]{3,2,1,0:T(8,128)S(1)} %get-tuple-element.46), channel_id=1, source_target_pairs={{16,0},{32,16},{48,32},{64,48},{80,64},{96,80},{112,96},{128,112},... | collective-permute-start | bytes 393224 | tf_op jit(solution)/shard_map/ppermute | solution.py:27
  26.6 6.4 %collective-permute-start.4 = (f32[8,10,1,256]{3,0,2,1:T(8,128)S(1)}, f32[8,10,1,256]{3,0,2,1:T(8,128)S(1)}, u32[]{:S(2)}, u32[]{:S(2)}) collective-permute-start(f32[8,10,1,256]{3,0,2,1:T(8,128)S(1)} %copy.466), channel_id=1, source_target_pairs={{1,0},{2,1},{3,2},{4,3},{5,4},{6,5},{7,6},{8,7},{9,8},{10,9},{11,1... | collective-permute-start | bytes 245768 | tf_op jit(solution)/shard_map/ppermute | solution.py:27
  28.6 5.1 %collective-permute-start.5 = (f32[8,10,1,256]{3,0,2,1:T(8,128)S(1)}, f32[8,10,1,256]{3,0,2,1:T(8,128)S(1)}, u32[]{:S(2)}, u32[]{:S(2)}) collective-permute-start(f32[8,10,1,256]{3,0,2,1:T(8,128)S(1)} %copy.467), channel_id=1, source_target_pairs={{0,1},{1,2},{2,3},{3,4},{4,5},{5,6},{6,7},{7,8},{8,9},{9,10},{10,1... | collective-permute-start | bytes 245768 | tf_op jit(solution)/shard_map/ppermute | solution.py:25
  33.8 84.3 %copy-start.5 = (f32[8,16,256]{2,1,0:T(8,128)S(1)}, f32[8,16,256]{2,1,0:T(8,128)}, u32[]{:S(2)}) copy-start(f32[8,16,256]{2,1,0:T(8,128)} %get-tuple-element.28) | copy-start | bytes 393220
  119.8 22.9 %copy-start.1 = (f32[8,8,16,256]{3,2,1,0:T(8,128)}, f32[8,8,16,256]{3,2,1,0:T(8,128)S(1)}, u32[]{:S(2)}) copy-start(f32[8,8,16,256]{3,2,1,0:T(8,128)S(1)} %get-tuple-element.26) | copy-start | bytes 3145732
  120.6 22.2 %collective-permute-start.6 = (f32[8,1,16,256]{3,2,1,0:T(8,128)}, f32[8,1,16,256]{3,2,1,0:T(8,128)S(1)}, u32[]{:S(2)}, u32[]{:S(2)}) collective-permute-start(f32[8,1,16,256]{3,2,1,0:T(8,128)} %get-tuple-element.45), channel_id=1, source_target_pairs={{16,0},{32,16},{48,32},{64,48},{80,64},{96,80},{112,96},{128,112},... | collective-permute-start | bytes 393224 | tf_op jit(solution)/shard_map/ppermute | solution.py:27
  121.8 20.9 %collective-permute-start.7 = (f32[8,1,16,256]{3,2,1,0:T(8,128)}, f32[8,1,16,256]{3,2,1,0:T(8,128)}, u32[]{:S(2)}, u32[]{:S(2)}) collective-permute-start(f32[8,1,16,256]{3,2,1,0:T(8,128)} %get-tuple-element.44), channel_id=1, source_target_pairs={{0,16},{16,32},{32,48},{48,64},{64,80},{80,96},{96,112},{112,128},... | collective-permute-start | bytes 393224 | tf_op jit(solution)/shard_map/ppermute | solution.py:25
  130.5 76.3 %collective-permute-start.14 = (f32[1,8,128]{2,1,0:T(8,128)}, f32[1,8,128]{2,1,0:T(8,128)}, u32[]{:S(2)}, u32[]{:S(2)}) collective-permute-start(f32[1,8,128]{2,1,0:T(8,128)} %slice.384), channel_id=1, source_target_pairs={{0,16},{16,32},{32,48},{48,64},{64,80},{80,96},{96,112},{112,128},... | collective-permute-start | bytes 12296 | tf_op jit(solution)/shard_map/ppermute | solution.py:14
  143.8 22.1 %collective-permute-start.8 = (f32[8,10,1,256]{3,0,2,1:T(8,128)S(1)}, f32[8,10,1,256]{3,0,2,1:T(8,128)S(1)}, u32[]{:S(2)}, u32[]{:S(2)}) collective-permute-start(f32[8,10,1,256]{3,0,2,1:T(8,128)S(1)} %copy.438), channel_id=1, source_target_pairs={{1,0},{2,1},{3,2},{4,3},{5,4},{6,5},{7,6},{8,7},{9,8},{10,9},{11,1... | collective-permute-start | bytes 245768 | tf_op jit(solution)/shard_map/ppermute | solution.py:27
  147.2 18.7 %collective-permute-start.9 = (f32[8,10,1,256]{3,0,2,1:T(8,128)S(1)}, f32[8,10,1,256]{3,0,2,1:T(8,128)S(1)}, u32[]{:S(2)}, u32[]{:S(2)}) collective-permute-start(f32[8,10,1,256]{3,0,2,1:T(8,128)S(1)} %copy.440), channel_id=1, source_target_pairs={{0,1},{1,2},{2,3},{3,4},{4,5},{5,6},{6,7},{7,8},{8,9},{9,10},{10,1... | collective-permute-start | bytes 245768 | tf_op jit(solution)/shard_map/ppermute | solution.py:25
  153.5 12.5 %copy-start.4 = (f32[8,16,256]{2,1,0:T(8,128)S(1)}, f32[8,16,256]{2,1,0:T(8,128)}, u32[]{:S(2)}) copy-start(f32[8,16,256]{2,1,0:T(8,128)} %copy-done.2) | copy-start | bytes 393220
  153.5 53.3 %collective-permute-start.15 = (f32[4,1,128]{2,1,0:T(1,128)}, f32[4,1,128]{2,1,0:T(1,128)}, u32[]{:S(2)}, u32[]{:S(2)}) collective-permute-start(f32[4,1,128]{2,1,0:T(1,128)} %slice.387), channel_id=1, source_target_pairs={{0,1},{1,2},{2,3},{3,4},{4,5},{5,6},{6,7},{7,8},{8,9},{9,10},{10,1... | collective-permute-start | bytes 6152 | tf_op jit(solution)/shard_map/ppermute | solution.py:14
  172.1 27.9 %collective-permute-start.10 = (f32[8,1,16,256]{3,2,1,0:T(8,128)}, f32[8,1,16,256]{3,2,1,0:T(8,128)}, u32[]{:S(2)}, u32[]{:S(2)}) collective-permute-start(f32[8,1,16,256]{3,2,1,0:T(8,128)} %get-tuple-element.43), channel_id=1, source_target_pairs={{16,0},{32,16},{48,32},{64,48},{80,64},{96,80},{112,96},{128,112},... | collective-permute-start | bytes 393224 | tf_op jit(solution)/shard_map/ppermute | solution.py:27
  173.4 26.6 %collective-permute-start.11 = (f32[8,1,16,256]{3,2,1,0:T(8,128)}, f32[8,1,16,256]{3,2,1,0:T(8,128)}, u32[]{:S(2)}, u32[]{:S(2)}) collective-permute-start(f32[8,1,16,256]{3,2,1,0:T(8,128)} %get-tuple-element.42), channel_id=1, source_target_pairs={{0,16},{16,32},{32,48},{48,64},{64,80},{80,96},{96,112},{112,128},... | collective-permute-start | bytes 393224 | tf_op jit(solution)/shard_map/ppermute | solution.py:25
  201.2 7.0 %collective-permute-start.12 = (f32[8,10,1,256]{3,0,2,1:T(8,128)S(1)}, f32[8,10,1,256]{3,0,2,1:T(8,128)S(1)}, u32[]{:S(2)}, u32[]{:S(2)}) collective-permute-start(f32[8,10,1,256]{3,0,2,1:T(8,128)S(1)} %copy.442), channel_id=1, source_target_pairs={{1,0},{2,1},{3,2},{4,3},{5,4},{6,5},{7,6},{8,7},{9,8},{10,9},{11,1... | collective-permute-start | bytes 245768 | tf_op jit(solution)/shard_map/ppermute | solution.py:27
  204.3 4.1 collective-permute-start.13
  237.0 31.6 %copy-start.10 = (f32[8,4,8,128]{3,2,1,0:T(8,128)S(1)}, f32[8,4,8,128]{3,2,1,0:T(8,128)}, u32[]{:S(2)}) copy-start(f32[8,4,8,128]{3,2,1,0:T(8,128)} %copy.447) | copy-start | bytes 393220
  237.0 31.6 %copy-start.22 = (f32[4,8,128]{2,1,0:T(8,128)S(1)}, f32[4,8,128]{2,1,0:T(8,128)}, u32[]{:S(2)}) copy-start(f32[4,8,128]{2,1,0:T(8,128)} %copy-done.20) | copy-start | bytes 49156
  237.0 31.6 %copy-start.24 = (f32[4,8,128]{2,1,0:T(8,128)S(1)}, f32[4,8,128]{2,1,0:T(8,128)}, u32[]{:S(2)}) copy-start(f32[4,8,128]{2,1,0:T(8,128)} %slice_reduce_fusion) | copy-start | bytes 49156
  237.0 31.6 %copy-start.29 = (f32[4,8,128]{2,1,0:T(8,128)S(1)}, f32[4,8,128]{2,1,0:T(8,128)}, u32[]{:S(2)}) copy-start(f32[4,8,128]{2,1,0:T(8,128)} %get-tuple-element.24) | copy-start | bytes 49156
  237.0 31.6 %copy-start.30 = (f32[4,8,128]{2,1,0:T(8,128)S(1)}, f32[4,8,128]{2,1,0:T(8,128)}, u32[]{:S(2)}) copy-start(f32[4,8,128]{2,1,0:T(8,128)} %get-tuple-element.25) | copy-start | bytes 49156
  237.0 31.6 %copy-start.31 = (f32[4,8,128]{2,1,0:T(8,128)S(1)}, f32[4,8,128]{2,1,0:T(8,128)}, u32[]{:S(2)}) copy-start(f32[4,8,128]{2,1,0:T(8,128)} %get-tuple-element.62) | copy-start | bytes 49156
  237.1 31.6 %copy-start.32 = (f32[4,8,128]{2,1,0:T(8,128)S(1)}, f32[4,8,128]{2,1,0:T(8,128)}, u32[]{:S(2)}) copy-start(f32[4,8,128]{2,1,0:T(8,128)} %get-tuple-element.63) | copy-start | bytes 49156
  238.1 5.3 %collective-permute-start.16 = (f32[8,1,8,128]{3,2,1,0:T(8,128)S(1)}, f32[8,1,8,128]{3,2,1,0:T(8,128)S(1)}, u32[]{:S(2)}, u32[]{:S(2)}) collective-permute-start(f32[8,1,8,128]{3,2,1,0:T(8,128)S(1)} %get-tuple-element.59), channel_id=1, source_target_pairs={{16,0},{32,16},{48,32},{64,48},{80,64},{96,80},{112,96},{128,112},... | collective-permute-start | bytes 98312 | tf_op jit(solution)/shard_map/ppermute | solution.py:27
  239.4 5.0 %collective-permute-start.17 = (f32[8,1,8,128]{3,2,1,0:T(8,128)S(1)}, f32[8,1,8,128]{3,2,1,0:T(8,128)S(1)}, u32[]{:S(2)}, u32[]{:S(2)}) collective-permute-start(f32[8,1,8,128]{3,2,1,0:T(8,128)S(1)} %get-tuple-element.58), channel_id=1, source_target_pairs={{0,16},{16,32},{32,48},{48,64},{64,80},{80,96},{96,112},{112,128},... | collective-permute-start | bytes 98312 | tf_op jit(solution)/shard_map/ppermute | solution.py:25
  244.4 7.3 %collective-permute-start.18 = (f32[8,6,1,128]{3,2,1,0:T(1,128)S(1)}, f32[8,6,1,128]{3,2,1,0:T(1,128)S(1)}, u32[]{:S(2)}, u32[]{:S(2)}) collective-permute-start(f32[8,6,1,128]{3,2,1,0:T(1,128)S(1)} %get-tuple-element.52), channel_id=1, source_target_pairs={{1,0},{2,1},{3,2},{4,3},{5,4},{6,5},{7,6},{8,7},{9,8},{10,9},{11,1... | collective-permute-start | bytes 73736 | tf_op jit(solution)/shard_map/ppermute | solution.py:27
  247.4 5.3 %collective-permute-start.19 = (f32[8,6,1,128]{3,2,1,0:T(1,128)S(1)}, f32[8,6,1,128]{3,2,1,0:T(1,128)S(1)}, u32[]{:S(2)}, u32[]{:S(2)}) collective-permute-start(f32[8,6,1,128]{3,2,1,0:T(1,128)S(1)} %get-tuple-element.53), channel_id=1, source_target_pairs={{0,1},{1,2},{2,3},{3,4},{4,5},{5,6},{6,7},{7,8},{8,9},{9,10},{10,1... | collective-permute-start | bytes 73736 | tf_op jit(solution)/shard_map/ppermute | solution.py:25
  253.8 5.9 %collective-permute-start.20 = (f32[8,1,8,128]{3,2,1,0:T(8,128)S(1)}, f32[8,1,8,128]{3,2,1,0:T(8,128)S(1)}, u32[]{:S(2)}, u32[]{:S(2)}) collective-permute-start(f32[8,1,8,128]{3,2,1,0:T(8,128)S(1)} %get-tuple-element.57), channel_id=1, source_target_pairs={{16,0},{32,16},{48,32},{64,48},{80,64},{96,80},{112,96},{128,112},... | collective-permute-start | bytes 98312 | tf_op jit(solution)/shard_map/ppermute | solution.py:27
  255.1 5.6 %collective-permute-start.21 = (f32[8,1,8,128]{3,2,1,0:T(8,128)S(1)}, f32[8,1,8,128]{3,2,1,0:T(8,128)S(1)}, u32[]{:S(2)}, u32[]{:S(2)}) collective-permute-start(f32[8,1,8,128]{3,2,1,0:T(8,128)S(1)} %get-tuple-element.56), channel_id=1, source_target_pairs={{0,16},{16,32},{32,48},{48,64},{64,80},{80,96},{96,112},{112,128},... | collective-permute-start | bytes 98312 | tf_op jit(solution)/shard_map/ppermute | solution.py:25
  260.7 7.0 %collective-permute-start.22 = (f32[8,6,1,128]{3,2,1,0:T(1,128)S(1)}, f32[8,6,1,128]{3,2,1,0:T(1,128)S(1)}, u32[]{:S(2)}, u32[]{:S(2)}) collective-permute-start(f32[8,6,1,128]{3,2,1,0:T(1,128)S(1)} %get-tuple-element.50), channel_id=1, source_target_pairs={{1,0},{2,1},{3,2},{4,3},{5,4},{6,5},{7,6},{8,7},{9,8},{10,9},{11,1... | collective-permute-start | bytes 73736 | tf_op jit(solution)/shard_map/ppermute | solution.py:27
  262.6 6.0 %collective-permute-start.23 = (f32[8,6,1,128]{3,2,1,0:T(1,128)S(1)}, f32[8,6,1,128]{3,2,1,0:T(1,128)S(1)}, u32[]{:S(2)}, u32[]{:S(2)}) collective-permute-start(f32[8,6,1,128]{3,2,1,0:T(1,128)S(1)} %get-tuple-element.51), channel_id=1, source_target_pairs={{0,1},{1,2},{2,3},{3,4},{4,5},{5,6},{6,7},{7,8},{8,9},{9,10},{10,1... | collective-permute-start | bytes 73736 | tf_op jit(solution)/shard_map/ppermute | solution.py:25
  268.8 5.9 %collective-permute-start.24 = (f32[8,1,8,128]{3,2,1,0:T(8,128)S(1)}, f32[8,1,8,128]{3,2,1,0:T(8,128)S(1)}, u32[]{:S(2)}, u32[]{:S(2)}) collective-permute-start(f32[8,1,8,128]{3,2,1,0:T(8,128)S(1)} %get-tuple-element.55), channel_id=1, source_target_pairs={{16,0},{32,16},{48,32},{64,48},{80,64},{96,80},{112,96},{128,112},... | collective-permute-start | bytes 98312 | tf_op jit(solution)/shard_map/ppermute | solution.py:27
  270.1 5.6 %collective-permute-start.25 = (f32[8,1,8,128]{3,2,1,0:T(8,128)S(1)}, f32[8,1,8,128]{3,2,1,0:T(8,128)S(1)}, u32[]{:S(2)}, u32[]{:S(2)}) collective-permute-start(f32[8,1,8,128]{3,2,1,0:T(8,128)S(1)} %get-tuple-element.54), channel_id=1, source_target_pairs={{0,16},{16,32},{32,48},{48,64},{64,80},{80,96},{96,112},{112,128},... | collective-permute-start | bytes 98312 | tf_op jit(solution)/shard_map/ppermute | solution.py:25
  275.8 7.0 %collective-permute-start.26 = (f32[8,6,1,128]{3,2,1,0:T(1,128)S(1)}, f32[8,6,1,128]{3,2,1,0:T(1,128)S(1)}, u32[]{:S(2)}, u32[]{:S(2)}) collective-permute-start(f32[8,6,1,128]{3,2,1,0:T(1,128)S(1)} %get-tuple-element.48), channel_id=1, source_target_pairs={{1,0},{2,1},{3,2},{4,3},{5,4},{6,5},{7,6},{8,7},{9,8},{10,9},{11,1... | collective-permute-start | bytes 73736 | tf_op jit(solution)/shard_map/ppermute | solution.py:27
  277.7 6.0 %collective-permute-start.27 = (f32[8,6,1,128]{3,2,1,0:T(1,128)S(1)}, f32[8,6,1,128]{3,2,1,0:T(1,128)S(1)}, u32[]{:S(2)}, u32[]{:S(2)}) collective-permute-start(f32[8,6,1,128]{3,2,1,0:T(1,128)S(1)} %get-tuple-element.49), channel_id=1, source_target_pairs={{0,1},{1,2},{2,3},{3,4},{4,5},{5,6},{6,7},{7,8},{8,9},{9,10},{10,1... | collective-permute-start | bytes 73736 | tf_op jit(solution)/shard_map/ppermute | solution.py:25
  306.5 16.7 %copy-start.7 = (f32[8,16,256]{2,1,0:T(8,128)S(1)}, f32[8,16,256]{2,1,0:T(8,128)}, u32[]{:S(2)}) copy-start(f32[8,16,256]{2,1,0:T(8,128)} %get-tuple-element.28) | copy-start | bytes 393220
  306.6 16.7 %copy-start.9 = (f32[8,16,256]{2,1,0:T(8,128)S(1)}, f32[8,16,256]{2,1,0:T(8,128)}, u32[]{:S(2)}) copy-start(f32[8,16,256]{2,1,0:T(8,128)} %copy-done.8) | copy-start | bytes 393220
  306.6 16.7 %copy-start.13 = (f32[8,16,256]{2,1,0:T(8,128)S(1)}, f32[8,16,256]{2,1,0:T(8,128)}, u32[]{:S(2)}) copy-start(f32[8,16,256]{2,1,0:T(8,128)} %copy-done.11) | copy-start | bytes 393220
  306.6 16.7 %copy-start.16 = (f32[8,16,256]{2,1,0:T(8,128)S(1)}, f32[8,16,256]{2,1,0:T(8,128)}, u32[]{:S(2)}) copy-start(f32[8,16,256]{2,1,0:T(8,128)} %copy-done.14) | copy-start | bytes 393220
  306.6 16.7 %copy-start.19 = (f32[8,16,256]{2,1,0:T(8,128)S(1)}, f32[8,16,256]{2,1,0:T(8,128)}, u32[]{:S(2)}) copy-start(f32[8,16,256]{2,1,0:T(8,128)} %copy-done.17) | copy-start | bytes 393220
  306.6 6.5 %collective-permute-start.28 = (f32[8,1,16,256]{3,2,1,0:T(8,128)S(1)}, f32[8,1,16,256]{3,2,1,0:T(8,128)S(1)}, u32[]{:S(2)}, u32[]{:S(2)}) collective-permute-start(f32[8,1,16,256]{3,2,1,0:T(8,128)S(1)} %get-tuple-element.41), channel_id=1, source_target_pairs={{16,0},{32,16},{48,32},{64,48},{80,64},{96,80},{112,96},{128,112},... | collective-permute-start | bytes 393224 | tf_op jit(solution)/shard_map/ppermute | solution.py:27
  308.1 6.5 %collective-permute-start.29 = (f32[8,1,16,256]{3,2,1,0:T(8,128)S(1)}, f32[8,1,16,256]{3,2,1,0:T(8,128)S(1)}, u32[]{:S(2)}, u32[]{:S(2)}) collective-permute-start(f32[8,1,16,256]{3,2,1,0:T(8,128)S(1)} %get-tuple-element.40), channel_id=1, source_target_pairs={{0,16},{16,32},{32,48},{48,64},{64,80},{80,96},{96,112},{112,128},... | collective-permute-start | bytes 393224 | tf_op jit(solution)/shard_map/ppermute | solution.py:25
  314.7 7.2 %collective-permute-start.30 = (f32[8,10,1,256]{3,0,2,1:T(8,128)S(1)}, f32[8,10,1,256]{3,0,2,1:T(8,128)S(1)}, u32[]{:S(2)}, u32[]{:S(2)}) collective-permute-start(f32[8,10,1,256]{3,0,2,1:T(8,128)S(1)} %copy.453), channel_id=1, source_target_pairs={{1,0},{2,1},{3,2},{4,3},{5,4},{6,5},{7,6},{8,7},{9,8},{10,9},{11,1... | collective-permute-start | bytes 245768 | tf_op jit(solution)/shard_map/ppermute | solution.py:27
  316.7 6.5 %collective-permute-start.31 = (f32[8,10,1,256]{3,0,2,1:T(8,128)S(1)}, f32[8,10,1,256]{3,0,2,1:T(8,128)S(1)}, u32[]{:S(2)}, u32[]{:S(2)}) collective-permute-start(f32[8,10,1,256]{3,0,2,1:T(8,128)S(1)} %copy.455), channel_id=1, source_target_pairs={{0,1},{1,2},{2,3},{3,4},{4,5},{5,6},{6,7},{7,8},{8,9},{9,10},{10,1... | collective-permute-start | bytes 245768 | tf_op jit(solution)/shard_map/ppermute | solution.py:25
  (21 other events, 130.1 us)
where the time goes:
time: 429 us; the launch traced here: 427 us
  blocking collectives  176 us (41%)
  starting transfers between devices  98.6 us (23%)
  local copies, waits for them, and re-layouts  80.4 us (19%)
  other arithmetic  57.3 us (13%)
  waiting for transfers between devices  9.35 us (2%)
    psum x1, blocking collectives, per_device(): gram = lax.psum(local_gram, ('gx', 'gy'))  93.9 us
    psum x1, blocking collectives, rayleigh_sums(): lax.psum((jnp.sum(vectors * applied, axis=(1, 2, 3)), jnp.sum(vectors * (...  82.2 us
    ppermute x14, starting transfers between devices, with_halo(): lax.ppermute(tail, axis, [(i, (i + 1) % count) for i in range(ends)])  59 us
    ppermute x14, starting transfers between devices, with_halo(): lax.ppermute(head, axis, [((i + 1) % count, i) for i in range(ends)])  26.2 us
    ppermute x4, starting transfers between devices, shifted(): return lax.ppermute(shard, axis, pairs)  13.3 us
    reduce_sum x1, other arithmetic, restrict(): field.reshape(kk, sx // 2, 2, sy // 2, 2, sz // 2, 2).sum(axis=(2, 4, 6))  13.1 us
    reshape x1, local copies, waits for them, and re-layouts, prolong(): jnp.broadcast_to(field[:, :, None, :, None, :, None], (kk, sx, 2, sy, 2,...  10.6 us
    reshape x1, local copies, waits for them, and re-layouts, coarse_weights(): dsum = degree.reshape(shape).sum(axis=(1, 3, 5))  10.5 us
  transfers between devices with their start and end apart: 32, of which 10 were waited for; matrix products, arithmetic and copies ran while one was open for 17% of the time, Pallas kernels for 0%

commit v1 on v0

--- a/solution.py
+++ b/solution.py
@@ -139,7 +139,7 @@
     local_gram = jnp.einsum(
         "aijk,bijk->ab", updated, degree[None] * updated, precision=lax.Precision.HIGHEST
     )
-    gram = lax.psum(local_gram, ("gx", "gy"))
+    gram = jnp.sum(lax.all_gather(local_gram, ("gx", "gy")), axis=0)
     gram = gram / (span_x * span_y * depth)
     chol = jnp.linalg.cholesky(gram)
     flat = updated.reshape(updated.shape[0], -1)

time: 429 us -> 415 us (0.967)
  blocking collectives: 176 us -> 162 us
    psum x1 -> x0, blocking collectives: 93.9 us -> none  [per_device(): gram = lax.psum(local_gram, ('gx', 'gy'))]
    all_gather x0 -> x1, blocking collectives: none -> 79.8 us  [per_device(): gram = jnp.sum(lax.all_gather(local_gram, ('gx', 'gy')), axis=0)]
where the time goes in v1:
time: 415 us; the launch traced here: 413 us
  blocking collectives  162 us (39%)
  starting transfers between devices  98.6 us (24%)
  local copies, waits for them, and re-layouts  80.4 us (19%)
  other arithmetic  57.3 us (14%)
  waiting for transfers between devices  9.35 us (2%)
    psum x1, blocking collectives, rayleigh_sums(): lax.psum((jnp.sum(vectors * applied, axis=(1, 2, 3)), jnp.sum(vectors * (...  82.2 us
    all_gather x1, blocking collectives, per_device(): gram = jnp.sum(lax.all_gather(local_gram, ('gx', 'gy')), axis=0)  79.8 us
    ppermute x14, starting transfers between devices, with_halo(): lax.ppermute(tail, axis, [(i, (i + 1) % count) for i in range(ends)])  59 us
    ppermute x14, starting transfers between devices, with_halo(): lax.ppermute(head, axis, [((i + 1) % count, i) for i in range(ends)])  26.2 us
    ppermute x4, starting transfers between devices, shifted(): return lax.ppermute(shard, axis, pairs)  13.3 us
    reduce_sum x1, other arithmetic, restrict(): field.reshape(kk, sx // 2, 2, sy // 2, 2, sz // 2, 2).sum(axis=(2, 4, 6))  13.1 us
    reshape x1, local copies, waits for them, and re-layouts, prolong(): jnp.broadcast_to(field[:, :, None, :, None, :, None], (kk, sx, 2, sy, 2,...  10.6 us
    reshape x1, local copies, waits for them, and re-layouts, coarse_weights(): dsum = degree.reshape(shape).sum(axis=(1, 3, 5))  10.5 us
  transfers between devices with their start and end apart: 32, of which 10 were waited for; matrix products, arithmetic and copies ran while one was open for 17% of the time, Pallas kernels for 0%

profile of v1, /device:TPU:1, one launch (start us, length us, event | category | flops | bytes accessed | tf_op | source)
XLA Modules:
  0.0 413.4 jit_solution(17687440952845115915)
XLA Ops:
  1.7 3.9 collective-permute-start
  6.6 4.4 %collective-permute-start.1 = (f32[8,1,256]{2,1,0:T(1,128)S(1)}, f32[8,1,256]{2,1,0:T(1,128)S(1)}, u32[]{:S(2)}, u32[]{:S(2)}) collective-permute-start(f32[8,1,256]{2,1,0:T(1,128)S(1)} %slice.374), channel_id=1, source_target_pairs={{0,1},{1,2},{2,3},{3,4},{4,5},{5,6},{6,7},{7,8},{8,9},{9,10},{10,1... | collective-permute-start | bytes 24584 | tf_op jit(solution)/shard_map/ppermute | solution.py:14
  12.0 3.1 collective-permute-start.3
  16.5 9.8 %reshape.74 = f32[4,2,8,2,128,2]{5,4,3,2,1,0:T(8,128)} reshape(f32[8,16,256]{2,1,0:T(8,128)S(1)} %broadcast_select_fusion.2) | data formatting | bytes 262144 | tf_op jit(solution)/shard_map/reshape | solution.py:90
  26.6 1.9 collective-permute-start.4
  28.6 3.6 collective-permute-start.5
  33.8 2.1 fusion
  35.9 82.2 %all-reduce.9 = (f32[8]{0:T(128)S(1)}, f32[8]{0:T(128)S(1)}) all-reduce(f32[8]{0:T(128)S(1)} %get-tuple-element.19, f32[8]{0:T(128)S(1)} %get-tuple-element.18), channel_id=1, replica_groups=mesh['gx'=16,'gy'=16] {'gx','gy'}, use_global_device_ids=true, to_apply=%region_1.2 | all-reduce | flops 16 | bytes 128 | tf_op jit(solution)/shard_map/psum | solution.py:78
  118.1 1.7 multiply_divide_fusion
  121.9 4.7 %collective-permute-start.7 = (f32[8,1,16,256]{3,2,1,0:T(8,128)}, f32[8,1,16,256]{3,2,1,0:T(8,128)}, u32[]{:S(2)}, u32[]{:S(2)}) collective-permute-start(f32[8,1,16,256]{3,2,1,0:T(8,128)} %get-tuple-element.44), channel_id=1, source_target_pairs={{0,16},{16,32},{32,48},{48,64},{64,80},{80,96},{96,112},{112,128},... | collective-permute-start | bytes 393224 | tf_op jit(solution)/shard_map/ppermute | solution.py:25
  126.5 2.8 slice_reduce_fusion.2
  130.5 2.5 collective-permute-start.14
  133.0 9.7 %reshape.75 = f32[4,2,8,2,128,2]{5,4,3,2,1,0:T(8,128)} reshape(f32[8,16,256]{2,1,0:T(8,128)S(1)} %broadcast_select_fusion.1) | data formatting | bytes 262144 | tf_op jit(solution)/shard_map/reshape | solution.py:91
  143.8 3.4 collective-permute-start.8
  147.3 2.9 collective-permute-start.9
  150.1 2.8 slice_reduce_fusion.1
  153.6 2.5 collective-permute-start.15
  156.1 9.8 %reshape.76 = f32[4,2,8,2,128,2]{5,4,3,2,1,0:T(8,128)} reshape(f32[8,16,256]{2,1,0:T(8,128)S(1)} %broadcast_select_fusion) | data formatting | bytes 262144 | tf_op jit(solution)/shard_map/reshape | solution.py:92
  166.1 5.0 %fusion.13 = f32[8,8,16,256]{3,2,1,0:T(8,128)S(1)} fusion(f32[8,8,16,256]{3,2,1,0:T(8,128)} %copy-done.1, f32[8,8,16,256]{3,2,1,0:T(8,128)S(1)} %get-tuple-element.27, f32[8,10,1,256]{3,2,1,0:T(1,128)S(1)} %copy.434, f32[8,1,16,256]{3,2,1,0:T(8,128)} %copy-done.25, f32[8,1,16,256]{3,2,1,0:T(8,128)} %collective-permute-done.7, ...), kind=kLoop, calls=%fused_computation.28 | loop fusion | flops 6553600 | bytes 4489216 | tf_op jit(solution)/shard_map/add | solution.py:72
  173.1 4.7 %collective-permute-start.11 = (f32[8,1,16,256]{3,2,1,0:T(8,128)}, f32[8,1,16,256]{3,2,1,0:T(8,128)}, u32[]{:S(2)}, u32[]{:S(2)}) collective-permute-start(f32[8,1,16,256]{3,2,1,0:T(8,128)} %get-tuple-element.42), channel_id=1, source_target_pairs={{0,16},{16,32},{32,48},{48,64},{64,80},{80,96},{96,112},{112,128},... | collective-permute-start | bytes 393224 | tf_op jit(solution)/shard_map/ppermute | solution.py:25
  177.7 6.8 %slice_reduce_fusion = f32[4,8,128]{2,1,0:T(8,128)} fusion(f32[4,2,8,2,128,2]{5,4,3,2,1,0:T(8,128)} %reshape.76), kind=kLoop, calls=%fused_computation | loop fusion | flops 12288 | bytes 81920 | tf_op jit(solution)/shard_map/reduce_sum | solution.py:92
  184.5 10.5 %reshape.77 = f32[4,2,8,2,128,2]{5,4,3,2,1,0:T(8,128)} reshape(f32[8,16,256]{2,1,0:T(8,128)} %copy-done.8) | data formatting | bytes 262144 | tf_op jit(solution)/shard_map/reshape | solution.py:93
  195.0 4.6 %reduce_sum.80 = f32[4,8,128]{2,1,0:T(8,128)} reduce(f32[4,2,8,2,128,2]{5,4,3,2,1,0:T(8,128)} %reshape.77, f32[]{:T(128)} %constant.66.clone.1), dimensions={1,3,5}, to_apply=%region_8.9 | reduce | flops 28672 | bytes 147460 | tf_op jit(solution)/shard_map/reduce_sum | solution.py:93
  200.9 3.0 collective-permute-start.12
  203.9 2.5 collective-permute-start.13
  208.1 2.8 fusion.19
  211.0 9.8 %copy.439 = f32[8,8,16,256]{0,3,2,1:T(8,128)} copy(f32[8,8,16,256]{3,2,1,0:T(8,128)} %fusion.19) | data formatting | bytes 2097152 | tf_op jit(solution)/shard_map/sub | solution.py:128
  220.8 13.1 %reduce_sum.76 = f32[8,4,8,128]{0,3,2,1:T(8,128)} reduce(f32[8,4,2,8,2,128,2]{0,6,5,4,3,2,1:T(2,128)} %bitcast.34, f32[]{:T(128)} %constant.66.clone.1), dimensions={2,4,6}, to_apply=%region_4.5 | reduce | flops 229376 | bytes 1179652 | tf_op jit(solution)/shard_map/reduce_sum | solution.py:99
  233.9 2.8 copy.440
  239.1 4.0 collective-permute-start.17
  244.1 2.9 collective-permute-start.18
  247.0 4.3 %collective-permute-start.19 = (f32[8,6,1,128]{3,2,1,0:T(1,128)S(1)}, f32[8,6,1,128]{3,2,1,0:T(1,128)S(1)}, u32[]{:S(2)}, u32[]{:S(2)}) collective-permute-start(f32[8,6,1,128]{3,2,1,0:T(1,128)S(1)} %get-tuple-element.53), channel_id=1, source_target_pairs={{0,1},{1,2},{2,3},{3,4},{4,5},{5,6},{6,7},{7,8},{8,9},{9,10},{10,1... | collective-permute-start | bytes 73736 | tf_op jit(solution)/shard_map/ppermute | solution.py:25
  254.7 4.6 %collective-permute-start.21 = (f32[8,1,8,128]{3,2,1,0:T(8,128)S(1)}, f32[8,1,8,128]{3,2,1,0:T(8,128)S(1)}, u32[]{:S(2)}, u32[]{:S(2)}) collective-permute-start(f32[8,1,8,128]{3,2,1,0:T(8,128)S(1)} %get-tuple-element.56), channel_id=1, source_target_pairs={{0,16},{16,32},{32,48},{48,64},{64,80},{80,96},{96,112},{112,128},... | collective-permute-start | bytes 98312 | tf_op jit(solution)/shard_map/ppermute | solution.py:25
  260.4 1.9 collective-permute-start.22
  262.3 5.1 %collective-permute-start.23 = (f32[8,6,1,128]{3,2,1,0:T(1,128)S(1)}, f32[8,6,1,128]{3,2,1,0:T(1,128)S(1)}, u32[]{:S(2)}, u32[]{:S(2)}) collective-permute-start(f32[8,6,1,128]{3,2,1,0:T(1,128)S(1)} %get-tuple-element.51), channel_id=1, source_target_pairs={{0,1},{1,2},{2,3},{3,4},{4,5},{5,6},{6,7},{7,8},{8,9},{9,10},{10,1... | collective-permute-start | bytes 73736 | tf_op jit(solution)/shard_map/ppermute | solution.py:25
  269.8 4.6 %collective-permute-start.25 = (f32[8,1,8,128]{3,2,1,0:T(8,128)S(1)}, f32[8,1,8,128]{3,2,1,0:T(8,128)S(1)}, u32[]{:S(2)}, u32[]{:S(2)}) collective-permute-start(f32[8,1,8,128]{3,2,1,0:T(8,128)S(1)} %get-tuple-element.54), channel_id=1, source_target_pairs={{0,16},{16,32},{32,48},{48,64},{64,80},{80,96},{96,112},{112,128},... | collective-permute-start | bytes 98312 | tf_op jit(solution)/shard_map/ppermute | solution.py:25
  275.4 1.9 collective-permute-start.26
  277.4 5.1 %collective-permute-start.27 = (f32[8,6,1,128]{3,2,1,0:T(1,128)S(1)}, f32[8,6,1,128]{3,2,1,0:T(1,128)S(1)}, u32[]{:S(2)}, u32[]{:S(2)}) collective-permute-start(f32[8,6,1,128]{3,2,1,0:T(1,128)S(1)} %get-tuple-element.49), channel_id=1, source_target_pairs={{0,1},{1,2},{2,3},{3,4},{4,5},{5,6},{6,7},{7,8},{8,9},{9,10},{10,1... | collective-permute-start | bytes 73736 | tf_op jit(solution)/shard_map/ppermute | solution.py:25
  284.2 2.9 copy.444
  287.0 7.1 %broadcast_in_dim.30 = f32[8,4,2,8,2,128,2]{0,6,5,4,3,2,1:T(2,128)} broadcast(f32[8,4,8,128]{0,3,2,1:T(8,128)} %copy.444), dimensions={0,1,3,5} | broadcast | bytes 1179648 | tf_op jit(solution)/shard_map/broadcast_in_dim | solution.py:104
  294.2 10.6 %copy.445 = f32[8,8,16,256]{3,2,1,0:T(8,128)} copy(f32[8,8,16,256]{0,3,2,1:T(8,128)} %bitcast.35) | data formatting | bytes 2097152 | tf_op jit(solution)/shard_map/reshape | solution.py:104
  307.7 4.6 %collective-permute-start.29 = (f32[8,1,16,256]{3,2,1,0:T(8,128)S(1)}, f32[8,1,16,256]{3,2,1,0:T(8,128)S(1)}, u32[]{:S(2)}, u32[]{:S(2)}) collective-permute-start(f32[8,1,16,256]{3,2,1,0:T(8,128)S(1)} %get-tuple-element.40), channel_id=1, source_target_pairs={{0,16},{16,32},{32,48},{48,64},{64,80},{80,96},{96,112},{112,128},... | collective-permute-start | bytes 393224 | tf_op jit(solution)/shard_map/ppermute | solution.py:25
  312.7 1.5 collective-permute-done.29
  314.4 1.9 collective-permute-start.30
  316.3 5.3 %collective-permute-start.31 = (f32[8,10,1,256]{3,0,2,1:T(8,128)S(1)}, f32[8,10,1,256]{3,0,2,1:T(8,128)S(1)}, u32[]{:S(2)}, u32[]{:S(2)}) collective-permute-start(f32[8,10,1,256]{3,0,2,1:T(8,128)S(1)} %copy.448), channel_id=1, source_target_pairs={{0,1},{1,2},{2,3},{3,4},{4,5},{5,6},{6,7},{7,8},{8,9},{9,10},{10,1... | collective-permute-start | bytes 245768 | tf_op jit(solution)/shard_map/ppermute | solution.py:25
  323.0 1.6 broadcast_multiply_fusion
  324.6 3.0 convolution_bitcast_fusion
  327.6 79.8 %all-gather = f32[2048,8]{1,0:T(8,128)S(1)} all-gather(f32[8,8]{1,0:T(8,128)S(1)} %convolution_bitcast_fusion), channel_id=2, replica_groups=mesh['gx'=16,'gy'=16] {'gx','gy'}, dimensions={0}, use_global_device_ids=true | all-gather | bytes 65792 | tf_op jit(solution)/shard_map/all_gather | solution.py:142
  (174 shorter events, 39.5 us)
Async XLA Ops:
  1.6 24.6 %copy-start.2 = (f32[8,16,256]{2,1,0:T(8,128)}, f32[8,16,256]{2,1,0:T(8,128)S(1)}, u32[]{:S(2)}) copy-start(f32[8,16,256]{2,1,0:T(8,128)S(1)} %broadcast_select_fusion.2) | copy-start | bytes 393220
  1.7 30.6 %collective-permute-start = (f32[1,16,256]{2,1,0:T(8,128)S(1)}, f32[1,16,256]{2,1,0:T(8,128)S(1)}, u32[]{:S(2)}, u32[]{:S(2)}) collective-permute-start(f32[1,16,256]{2,1,0:T(8,128)S(1)} %slice.372), channel_id=1, source_target_pairs={{0,16},{16,32},{32,48},{48,64},{64,80},{80,96},{96,112},{112,128},... | collective-permute-start | bytes 49160 | tf_op jit(solution)/shard_map/ppermute | solution.py:14
  6.6 25.6 %collective-permute-start.1 = (f32[8,1,256]{2,1,0:T(1,128)S(1)}, f32[8,1,256]{2,1,0:T(1,128)S(1)}, u32[]{:S(2)}, u32[]{:S(2)}) collective-permute-start(f32[8,1,256]{2,1,0:T(1,128)S(1)} %slice.374), channel_id=1, source_target_pairs={{0,1},{1,2},{2,3},{3,4},{4,5},{5,6},{6,7},{7,8},{8,9},{9,10},{10,1... | collective-permute-start | bytes 24584 | tf_op jit(solution)/shard_map/ppermute | solution.py:14
  12.0 14.3 %collective-permute-start.3 = (f32[8,1,16,256]{3,2,1,0:T(8,128)S(1)}, f32[8,1,16,256]{3,2,1,0:T(8,128)S(1)}, u32[]{:S(2)}, u32[]{:S(2)}) collective-permute-start(f32[8,1,16,256]{3,2,1,0:T(8,128)S(1)} %get-tuple-element.47), channel_id=1, source_target_pairs={{0,16},{16,32},{32,48},{48,64},{64,80},{80,96},{96,112},{112,128},... | collective-permute-start | bytes 393224 | tf_op jit(solution)/shard_map/ppermute | solution.py:25
  15.2 11.3 %collective-permute-start.2 = (f32[8,1,16,256]{3,2,1,0:T(8,128)S(1)}, f32[8,1,16,256]{3,2,1,0:T(8,128)S(1)}, u32[]{:S(2)}, u32[]{:S(2)}) collective-permute-start(f32[8,1,16,256]{3,2,1,0:T(8,128)S(1)} %get-tuple-element.46), channel_id=1, source_target_pairs={{16,0},{32,16},{48,32},{64,48},{80,64},{96,80},{112,96},{128,112},... | collective-permute-start | bytes 393224 | tf_op jit(solution)/shard_map/ppermute | solution.py:27
  26.6 6.4 %collective-permute-start.4 = (f32[8,10,1,256]{3,0,2,1:T(8,128)S(1)}, f32[8,10,1,256]{3,0,2,1:T(8,128)S(1)}, u32[]{:S(2)}, u32[]{:S(2)}) collective-permute-start(f32[8,10,1,256]{3,0,2,1:T(8,128)S(1)} %copy.457), channel_id=1, source_target_pairs={{1,0},{2,1},{3,2},{4,3},{5,4},{6,5},{7,6},{8,7},{9,8},{10,9},{11,1... | collective-permute-start | bytes 245768 | tf_op jit(solution)/shard_map/ppermute | solution.py:27
  28.6 5.1 %collective-permute-start.5 = (f32[8,10,1,256]{3,0,2,1:T(8,128)S(1)}, f32[8,10,1,256]{3,0,2,1:T(8,128)S(1)}, u32[]{:S(2)}, u32[]{:S(2)}) collective-permute-start(f32[8,10,1,256]{3,0,2,1:T(8,128)S(1)} %copy.458), channel_id=1, source_target_pairs={{0,1},{1,2},{2,3},{3,4},{4,5},{5,6},{6,7},{7,8},{8,9},{9,10},{10,1... | collective-permute-start | bytes 245768 | tf_op jit(solution)/shard_map/ppermute | solution.py:25
  33.8 84.3 %copy-start.5 = (f32[8,16,256]{2,1,0:T(8,128)S(1)}, f32[8,16,256]{2,1,0:T(8,128)}, u32[]{:S(2)}) copy-start(f32[8,16,256]{2,1,0:T(8,128)} %get-tuple-element.28) | copy-start | bytes 393220
  119.8 22.9 %copy-start.1 = (f32[8,8,16,256]{3,2,1,0:T(8,128)}, f32[8,8,16,256]{3,2,1,0:T(8,128)S(1)}, u32[]{:S(2)}) copy-start(f32[8,8,16,256]{3,2,1,0:T(8,128)S(1)} %get-tuple-element.26) | copy-start | bytes 3145732
  120.6 22.2 %collective-permute-start.6 = (f32[8,1,16,256]{3,2,1,0:T(8,128)}, f32[8,1,16,256]{3,2,1,0:T(8,128)S(1)}, u32[]{:S(2)}, u32[]{:S(2)}) collective-permute-start(f32[8,1,16,256]{3,2,1,0:T(8,128)} %get-tuple-element.45), channel_id=1, source_target_pairs={{16,0},{32,16},{48,32},{64,48},{80,64},{96,80},{112,96},{128,112},... | collective-permute-start | bytes 393224 | tf_op jit(solution)/shard_map/ppermute | solution.py:27
  121.9 20.9 %collective-permute-start.7 = (f32[8,1,16,256]{3,2,1,0:T(8,128)}, f32[8,1,16,256]{3,2,1,0:T(8,128)}, u32[]{:S(2)}, u32[]{:S(2)}) collective-permute-start(f32[8,1,16,256]{3,2,1,0:T(8,128)} %get-tuple-element.44), channel_id=1, source_target_pairs={{0,16},{16,32},{32,48},{48,64},{64,80},{80,96},{96,112},{112,128},... | collective-permute-start | bytes 393224 | tf_op jit(solution)/shard_map/ppermute | solution.py:25
  130.5 76.0 %collective-permute-start.14 = (f32[1,8,128]{2,1,0:T(8,128)}, f32[1,8,128]{2,1,0:T(8,128)}, u32[]{:S(2)}, u32[]{:S(2)}) collective-permute-start(f32[1,8,128]{2,1,0:T(8,128)} %slice.384), channel_id=1, source_target_pairs={{0,16},{16,32},{32,48},{48,64},{64,80},{80,96},{96,112},{112,128},... | collective-permute-start | bytes 12296 | tf_op jit(solution)/shard_map/ppermute | solution.py:14
  143.8 22.1 %collective-permute-start.8 = (f32[8,10,1,256]{3,0,2,1:T(8,128)S(1)}, f32[8,10,1,256]{3,0,2,1:T(8,128)S(1)}, u32[]{:S(2)}, u32[]{:S(2)}) collective-permute-start(f32[8,10,1,256]{3,0,2,1:T(8,128)S(1)} %copy.431), channel_id=1, source_target_pairs={{1,0},{2,1},{3,2},{4,3},{5,4},{6,5},{7,6},{8,7},{9,8},{10,9},{11,1... | collective-permute-start | bytes 245768 | tf_op jit(solution)/shard_map/ppermute | solution.py:27
  147.3 18.7 %collective-permute-start.9 = (f32[8,10,1,256]{3,0,2,1:T(8,128)S(1)}, f32[8,10,1,256]{3,0,2,1:T(8,128)S(1)}, u32[]{:S(2)}, u32[]{:S(2)}) collective-permute-start(f32[8,10,1,256]{3,0,2,1:T(8,128)S(1)} %copy.433), channel_id=1, source_target_pairs={{0,1},{1,2},{2,3},{3,4},{4,5},{5,6},{6,7},{7,8},{8,9},{9,10},{10,1... | collective-permute-start | bytes 245768 | tf_op jit(solution)/shard_map/ppermute | solution.py:25
  153.6 12.5 %copy-start.4 = (f32[8,16,256]{2,1,0:T(8,128)S(1)}, f32[8,16,256]{2,1,0:T(8,128)}, u32[]{:S(2)}) copy-start(f32[8,16,256]{2,1,0:T(8,128)} %copy-done.2) | copy-start | bytes 393220
  153.6 52.9 %collective-permute-start.15 = (f32[4,1,128]{2,1,0:T(1,128)}, f32[4,1,128]{2,1,0:T(1,128)}, u32[]{:S(2)}, u32[]{:S(2)}) collective-permute-start(f32[4,1,128]{2,1,0:T(1,128)} %slice.387), channel_id=1, source_target_pairs={{0,1},{1,2},{2,3},{3,4},{4,5},{5,6},{6,7},{7,8},{8,9},{9,10},{10,1... | collective-permute-start | bytes 6152 | tf_op jit(solution)/shard_map/ppermute | solution.py:14
  171.8 27.9 %collective-permute-start.10 = (f32[8,1,16,256]{3,2,1,0:T(8,128)}, f32[8,1,16,256]{3,2,1,0:T(8,128)}, u32[]{:S(2)}, u32[]{:S(2)}) collective-permute-start(f32[8,1,16,256]{3,2,1,0:T(8,128)} %get-tuple-element.43), channel_id=1, source_target_pairs={{16,0},{32,16},{48,32},{64,48},{80,64},{96,80},{112,96},{128,112},... | collective-permute-start | bytes 393224 | tf_op jit(solution)/shard_map/ppermute | solution.py:27
  173.1 26.6 %collective-permute-start.11 = (f32[8,1,16,256]{3,2,1,0:T(8,128)}, f32[8,1,16,256]{3,2,1,0:T(8,128)}, u32[]{:S(2)}, u32[]{:S(2)}) collective-permute-start(f32[8,1,16,256]{3,2,1,0:T(8,128)} %get-tuple-element.42), channel_id=1, source_target_pairs={{0,16},{16,32},{32,48},{48,64},{64,80},{80,96},{96,112},{112,128},... | collective-permute-start | bytes 393224 | tf_op jit(solution)/shard_map/ppermute | solution.py:25
  200.9 7.0 %collective-permute-start.12 = (f32[8,10,1,256]{3,0,2,1:T(8,128)S(1)}, f32[8,10,1,256]{3,0,2,1:T(8,128)S(1)}, u32[]{:S(2)}, u32[]{:S(2)}) collective-permute-start(f32[8,10,1,256]{3,0,2,1:T(8,128)S(1)} %copy.435), channel_id=1, source_target_pairs={{1,0},{2,1},{3,2},{4,3},{5,4},{6,5},{7,6},{8,7},{9,8},{10,9},{11,1... | collective-permute-start | bytes 245768 | tf_op jit(solution)/shard_map/ppermute | solution.py:27
  203.9 4.1 collective-permute-start.13
  236.7 31.6 %copy-start.10 = (f32[8,4,8,128]{3,2,1,0:T(8,128)S(1)}, f32[8,4,8,128]{3,2,1,0:T(8,128)}, u32[]{:S(2)}) copy-start(f32[8,4,8,128]{3,2,1,0:T(8,128)} %copy.440) | copy-start | bytes 393220
  236.7 31.6 %copy-start.22 = (f32[4,8,128]{2,1,0:T(8,128)S(1)}, f32[4,8,128]{2,1,0:T(8,128)}, u32[]{:S(2)}) copy-start(f32[4,8,128]{2,1,0:T(8,128)} %copy-done.20) | copy-start | bytes 49156
  236.7 31.6 %copy-start.24 = (f32[4,8,128]{2,1,0:T(8,128)S(1)}, f32[4,8,128]{2,1,0:T(8,128)}, u32[]{:S(2)}) copy-start(f32[4,8,128]{2,1,0:T(8,128)} %slice_reduce_fusion) | copy-start | bytes 49156
  236.7 31.6 %copy-start.29 = (f32[4,8,128]{2,1,0:T(8,128)S(1)}, f32[4,8,128]{2,1,0:T(8,128)}, u32[]{:S(2)}) copy-start(f32[4,8,128]{2,1,0:T(8,128)} %get-tuple-element.24) | copy-start | bytes 49156
  236.7 31.6 %copy-start.30 = (f32[4,8,128]{2,1,0:T(8,128)S(1)}, f32[4,8,128]{2,1,0:T(8,128)}, u32[]{:S(2)}) copy-start(f32[4,8,128]{2,1,0:T(8,128)} %get-tuple-element.25) | copy-start | bytes 49156
  236.7 31.6 %copy-start.31 = (f32[4,8,128]{2,1,0:T(8,128)S(1)}, f32[4,8,128]{2,1,0:T(8,128)}, u32[]{:S(2)}) copy-start(f32[4,8,128]{2,1,0:T(8,128)} %get-tuple-element.62) | copy-start | bytes 49156
  236.7 31.6 %copy-start.32 = (f32[4,8,128]{2,1,0:T(8,128)S(1)}, f32[4,8,128]{2,1,0:T(8,128)}, u32[]{:S(2)}) copy-start(f32[4,8,128]{2,1,0:T(8,128)} %get-tuple-element.63) | copy-start | bytes 49156
  237.8 5.3 %collective-permute-start.16 = (f32[8,1,8,128]{3,2,1,0:T(8,128)S(1)}, f32[8,1,8,128]{3,2,1,0:T(8,128)S(1)}, u32[]{:S(2)}, u32[]{:S(2)}) collective-permute-start(f32[8,1,8,128]{3,2,1,0:T(8,128)S(1)} %get-tuple-element.59), channel_id=1, source_target_pairs={{16,0},{32,16},{48,32},{64,48},{80,64},{96,80},{112,96},{128,112},... | collective-permute-start | bytes 98312 | tf_op jit(solution)/shard_map/ppermute | solution.py:27
  239.1 5.0 %collective-permute-start.17 = (f32[8,1,8,128]{3,2,1,0:T(8,128)S(1)}, f32[8,1,8,128]{3,2,1,0:T(8,128)S(1)}, u32[]{:S(2)}, u32[]{:S(2)}) collective-permute-start(f32[8,1,8,128]{3,2,1,0:T(8,128)S(1)} %get-tuple-element.58), channel_id=1, source_target_pairs={{0,16},{16,32},{32,48},{48,64},{64,80},{80,96},{96,112},{112,128},... | collective-permute-start | bytes 98312 | tf_op jit(solution)/shard_map/ppermute | solution.py:25
  244.1 7.3 %collective-permute-start.18 = (f32[8,6,1,128]{3,2,1,0:T(1,128)S(1)}, f32[8,6,1,128]{3,2,1,0:T(1,128)S(1)}, u32[]{:S(2)}, u32[]{:S(2)}) collective-permute-start(f32[8,6,1,128]{3,2,1,0:T(1,128)S(1)} %get-tuple-element.52), channel_id=1, source_target_pairs={{1,0},{2,1},{3,2},{4,3},{5,4},{6,5},{7,6},{8,7},{9,8},{10,9},{11,1... | collective-permute-start | bytes 73736 | tf_op jit(solution)/shard_map/ppermute | solution.py:27
  247.0 5.3 %collective-permute-start.19 = (f32[8,6,1,128]{3,2,1,0:T(1,128)S(1)}, f32[8,6,1,128]{3,2,1,0:T(1,128)S(1)}, u32[]{:S(2)}, u32[]{:S(2)}) collective-permute-start(f32[8,6,1,128]{3,2,1,0:T(1,128)S(1)} %get-tuple-element.53), channel_id=1, source_target_pairs={{0,1},{1,2},{2,3},{3,4},{4,5},{5,6},{6,7},{7,8},{8,9},{9,10},{10,1... | collective-permute-start | bytes 73736 | tf_op jit(solution)/shard_map/ppermute | solution.py:25
  253.4 5.9 %collective-permute-start.20 = (f32[8,1,8,128]{3,2,1,0:T(8,128)S(1)}, f32[8,1,8,128]{3,2,1,0:T(8,128)S(1)}, u32[]{:S(2)}, u32[]{:S(2)}) collective-permute-start(f32[8,1,8,128]{3,2,1,0:T(8,128)S(1)} %get-tuple-element.57), channel_id=1, source_target_pairs={{16,0},{32,16},{48,32},{64,48},{80,64},{96,80},{112,96},{128,112},... | collective-permute-start | bytes 98312 | tf_op jit(solution)/shard_map/ppermute | solution.py:27
  254.7 5.6 %collective-permute-start.21 = (f32[8,1,8,128]{3,2,1,0:T(8,128)S(1)}, f32[8,1,8,128]{3,2,1,0:T(8,128)S(1)}, u32[]{:S(2)}, u32[]{:S(2)}) collective-permute-start(f32[8,1,8,128]{3,2,1,0:T(8,128)S(1)} %get-tuple-element.56), channel_id=1, source_target_pairs={{0,16},{16,32},{32,48},{48,64},{64,80},{80,96},{96,112},{112,128},... | collective-permute-start | bytes 98312 | tf_op jit(solution)/shard_map/ppermute | solution.py:25
  260.4 7.0 %collective-permute-start.22 = (f32[8,6,1,128]{3,2,1,0:T(1,128)S(1)}, f32[8,6,1,128]{3,2,1,0:T(1,128)S(1)}, u32[]{:S(2)}, u32[]{:S(2)}) collective-permute-start(f32[8,6,1,128]{3,2,1,0:T(1,128)S(1)} %get-tuple-element.50), channel_id=1, source_target_pairs={{1,0},{2,1},{3,2},{4,3},{5,4},{6,5},{7,6},{8,7},{9,8},{10,9},{11,1... | collective-permute-start | bytes 73736 | tf_op jit(solution)/shard_map/ppermute | solution.py:27
  262.3 6.0 %collective-permute-start.23 = (f32[8,6,1,128]{3,2,1,0:T(1,128)S(1)}, f32[8,6,1,128]{3,2,1,0:T(1,128)S(1)}, u32[]{:S(2)}, u32[]{:S(2)}) collective-permute-start(f32[8,6,1,128]{3,2,1,0:T(1,128)S(1)} %get-tuple-element.51), channel_id=1, source_target_pairs={{0,1},{1,2},{2,3},{3,4},{4,5},{5,6},{6,7},{7,8},{8,9},{9,10},{10,1... | collective-permute-start | bytes 73736 | tf_op jit(solution)/shard_map/ppermute | solution.py:25
  268.5 5.9 %collective-permute-start.24 = (f32[8,1,8,128]{3,2,1,0:T(8,128)S(1)}, f32[8,1,8,128]{3,2,1,0:T(8,128)S(1)}, u32[]{:S(2)}, u32[]{:S(2)}) collective-permute-start(f32[8,1,8,128]{3,2,1,0:T(8,128)S(1)} %get-tuple-element.55), channel_id=1, source_target_pairs={{16,0},{32,16},{48,32},{64,48},{80,64},{96,80},{112,96},{128,112},... | collective-permute-start | bytes 98312 | tf_op jit(solution)/shard_map/ppermute | solution.py:27
  269.8 5.6 %collective-permute-start.25 = (f32[8,1,8,128]{3,2,1,0:T(8,128)S(1)}, f32[8,1,8,128]{3,2,1,0:T(8,128)S(1)}, u32[]{:S(2)}, u32[]{:S(2)}) collective-permute-start(f32[8,1,8,128]{3,2,1,0:T(8,128)S(1)} %get-tuple-element.54), channel_id=1, source_target_pairs={{0,16},{16,32},{32,48},{48,64},{64,80},{80,96},{96,112},{112,128},... | collective-permute-start | bytes 98312 | tf_op jit(solution)/shard_map/ppermute | solution.py:25
  275.4 7.0 %collective-permute-start.26 = (f32[8,6,1,128]{3,2,1,0:T(1,128)S(1)}, f32[8,6,1,128]{3,2,1,0:T(1,128)S(1)}, u32[]{:S(2)}, u32[]{:S(2)}) collective-permute-start(f32[8,6,1,128]{3,2,1,0:T(1,128)S(1)} %get-tuple-element.48), channel_id=1, source_target_pairs={{1,0},{2,1},{3,2},{4,3},{5,4},{6,5},{7,6},{8,7},{9,8},{10,9},{11,1... | collective-permute-start | bytes 73736 | tf_op jit(solution)/shard_map/ppermute | solution.py:27
  277.4 6.0 %collective-permute-start.27 = (f32[8,6,1,128]{3,2,1,0:T(1,128)S(1)}, f32[8,6,1,128]{3,2,1,0:T(1,128)S(1)}, u32[]{:S(2)}, u32[]{:S(2)}) collective-permute-start(f32[8,6,1,128]{3,2,1,0:T(1,128)S(1)} %get-tuple-element.49), channel_id=1, source_target_pairs={{0,1},{1,2},{2,3},{3,4},{4,5},{5,6},{6,7},{7,8},{8,9},{9,10},{10,1... | collective-permute-start | bytes 73736 | tf_op jit(solution)/shard_map/ppermute | solution.py:25
  306.2 16.7 %copy-start.7 = (f32[8,16,256]{2,1,0:T(8,128)S(1)}, f32[8,16,256]{2,1,0:T(8,128)}, u32[]{:S(2)}) copy-start(f32[8,16,256]{2,1,0:T(8,128)} %get-tuple-element.28) | copy-start | bytes 393220
  306.2 16.7 %copy-start.9 = (f32[8,16,256]{2,1,0:T(8,128)S(1)}, f32[8,16,256]{2,1,0:T(8,128)}, u32[]{:S(2)}) copy-start(f32[8,16,256]{2,1,0:T(8,128)} %copy-done.8) | copy-start | bytes 393220
  306.2 16.7 %copy-start.13 = (f32[8,16,256]{2,1,0:T(8,128)S(1)}, f32[8,16,256]{2,1,0:T(8,128)}, u32[]{:S(2)}) copy-start(f32[8,16,256]{2,1,0:T(8,128)} %copy-done.11) | copy-start | bytes 393220
  306.2 16.7 %copy-start.16 = (f32[8,16,256]{2,1,0:T(8,128)S(1)}, f32[8,16,256]{2,1,0:T(8,128)}, u32[]{:S(2)}) copy-start(f32[8,16,256]{2,1,0:T(8,128)} %copy-done.14) | copy-start | bytes 393220
  306.2 16.7 %copy-start.19 = (f32[8,16,256]{2,1,0:T(8,128)S(1)}, f32[8,16,256]{2,1,0:T(8,128)}, u32[]{:S(2)}) copy-start(f32[8,16,256]{2,1,0:T(8,128)} %copy-done.17) | copy-start | bytes 393220
  306.3 6.5 %collective-permute-start.28 = (f32[8,1,16,256]{3,2,1,0:T(8,128)S(1)}, f32[8,1,16,256]{3,2,1,0:T(8,128)S(1)}, u32[]{:S(2)}, u32[]{:S(2)}) collective-permute-start(f32[8,1,16,256]{3,2,1,0:T(8,128)S(1)} %get-tuple-element.41), channel_id=1, source_target_pairs={{16,0},{32,16},{48,32},{64,48},{80,64},{96,80},{112,96},{128,112},... | collective-permute-start | bytes 393224 | tf_op jit(solution)/shard_map/ppermute | solution.py:27
  307.7 6.5 %collective-permute-start.29 = (f32[8,1,16,256]{3,2,1,0:T(8,128)S(1)}, f32[8,1,16,256]{3,2,1,0:T(8,128)S(1)}, u32[]{:S(2)}, u32[]{:S(2)}) collective-permute-start(f32[8,1,16,256]{3,2,1,0:T(8,128)S(1)} %get-tuple-element.40), channel_id=1, source_target_pairs={{0,16},{16,32},{32,48},{48,64},{64,80},{80,96},{96,112},{112,128},... | collective-permute-start | bytes 393224 | tf_op jit(solution)/shard_map/ppermute | solution.py:25
  314.4 7.2 %collective-permute-start.30 = (f32[8,10,1,256]{3,0,2,1:T(8,128)S(1)}, f32[8,10,1,256]{3,0,2,1:T(8,128)S(1)}, u32[]{:S(2)}, u32[]{:S(2)}) collective-permute-start(f32[8,10,1,256]{3,0,2,1:T(8,128)S(1)} %copy.446), channel_id=1, source_target_pairs={{1,0},{2,1},{3,2},{4,3},{5,4},{6,5},{7,6},{8,7},{9,8},{10,9},{11,1... | collective-permute-start | bytes 245768 | tf_op jit(solution)/shard_map/ppermute | solution.py:27
  316.3 6.5 %collective-permute-start.31 = (f32[8,10,1,256]{3,0,2,1:T(8,128)S(1)}, f32[8,10,1,256]{3,0,2,1:T(8,128)S(1)}, u32[]{:S(2)}, u32[]{:S(2)}) collective-permute-start(f32[8,10,1,256]{3,0,2,1:T(8,128)S(1)} %copy.448), channel_id=1, source_target_pairs={{0,1},{1,2},{2,3},{3,4},{4,5},{5,6},{6,7},{7,8},{8,9},{9,10},{10,1... | collective-permute-start | bytes 245768 | tf_op jit(solution)/shard_map/ppermute | solution.py:25
  (21 other events, 130.1 us)
